TPU v7x, 128 devices: a whole 4x4x4 slice. The times are simulated.
128 devices in a mesh: ctx: 16 (over z_lo, y, core), tp: 4 (over x), grp: 2 (over z_hi).
Axes of the slice: x: 4, y: 4, z: 4 (z_hi: 2, z_lo: 2; z = z_hi * 2 + z_lo), core: 2. Of those that a mesh axis runs over, the one named last changes fastest.
Arguments:
- new_tokens: bfloat16 [2, 512, 4608], P('grp', None, 'ctx'), may hold values from -6 to 6
- w_query: bfloat16 [4608, 4096], P('ctx', 'tp'), may hold values from -0.25 to 0.25
- w_key: bfloat16 [4608, 2048], P('ctx', 'tp'), may hold values from -0.09375 to 0.09375
- w_value: bfloat16 [4608, 2048], P('ctx', 'tp'), may hold values from -0.09375 to 0.09375
- w_out: bfloat16 [4096, 4608], P('tp', 'ctx'), may hold values from -0.25 to 0.25
- pool_keys: bfloat16 [2, 81920, 16, 128], P('grp', 'ctx', 'tp'), may hold values from -6 to 6
- pool_values: bfloat16 [2, 81920, 16, 128], P('grp', 'ctx', 'tp'), may hold values from -6 to 6
- stretch_start: int32 [1], replicated, may hold values from 40960 to 81408
- lengths: int32 [8], replicated, may hold values from 1 to 9216, as said below
- dest_blocks: int32 [32], replicated, may hold values from 288 to 5119, as said below
Outputs:
- attn_out: bfloat16 [2, 512, 4608], P('grp', 'tp', 'ctx')
- keys_out: bfloat16 [2, 81920, 16, 128], P('grp', 'ctx', 'tp')
- values_out: bfloat16 [2, 81920, 16, 128], P('grp', 'ctx', 'tp')
Inputs may be any that keep to these rules, and one draw needn't show every extreme that they name: `lengths`: the longest context is exactly 9216 in every draw, and some request has length 1. `dest_blocks`: the entries are distinct. Each block lies in the last 512 slots of its index of ctx, that is j % 5120 >= 4608 for its slots j, so no request reads it; both the first and the last such block of the pool are always named.
All inputs are finite; a program needn't handle non-finite values.
Results may differ from a plain program's by a relative error of at most 0.014.
Values may be sent and summed in bfloat16 or wider, within the bound.
A program may use at most 128 MiB of HBM per device.

v0:
```python
import math

import jax
import jax.numpy as jnp
from jax import lax
from jax.sharding import PartitionSpec as P

HQ = 32
KVH = 16
HD = 128
BLK = 16


soft_cap = 50.0
query_scale = 1.0 / 12.0


def passed_along(value, axis, steps):
    count = lax.axis_size(axis)
    leading, last = (max(0, -steps), min(count, count - steps))
    return lax.ppermute(value, axis, [(source, source + steps) for source in range(leading, last)])


def weights_of(scores, valid):
    capped = soft_cap * jnp.tanh(scores / soft_cap)
    return jnp.where(valid, jnp.exp(capped), 0.0).astype(jnp.bfloat16)


def prefix_local(queries, key_rows, value_rows, stretch_first, first_slot):
    slot_count = key_rows.shape[0]
    block_rows = math.gcd(slot_count, 512)
    block_count = slot_count // block_rows
    key_blocks = key_rows.reshape(block_count, block_rows, key_rows.shape[1], key_rows.shape[2])
    value_blocks = value_rows.reshape(
        block_count, block_rows, value_rows.shape[1], value_rows.shape[2]
    )
    numerator = jnp.zeros(queries.shape, jnp.float32)
    denominator = jnp.zeros(queries.shape[:3], jnp.float32)

    def advance(totals, members):
        numerator, denominator = totals
        key_block, value_block, block_index = members
        position = first_slot + block_index * block_rows + jnp.arange(block_rows, dtype=jnp.int32)
        scores = jnp.einsum(
            "rkgd,jkd->rkgj", queries, key_block, preferred_element_type=jnp.float32
        )
        weights = weights_of(scores, (position < stretch_first)[None, None, None, :])
        numerator = numerator + jnp.einsum(
            "rkgj,jkd->rkgd", weights, value_block, preferred_element_type=jnp.float32
        )
        denominator = denominator + jnp.sum(weights.astype(jnp.float32), axis=-1)
        return ((numerator, denominator), None)

    (numerator, denominator), leftover = lax.scan(
        advance,
        (numerator, denominator),
        (key_blocks, value_blocks, jnp.arange(block_count, dtype=jnp.int32)),
    )
    return (numerator, denominator)


def cache_local(queries, key_rows, value_rows, lengths, ctx_index, ctx_count):
    row_total = queries.shape[0]
    request_count = lengths.shape[0]
    spec_rows = row_total // request_count
    kv_heads = queries.shape[1]
    grouped = queries.shape[2]
    planes = key_rows.shape[0] // request_count
    key_grid = key_rows.reshape(planes, request_count, key_rows.shape[1], key_rows.shape[2])
    value_grid = value_rows.reshape(planes, request_count, value_rows.shape[1], value_rows.shape[2])
    request_q = queries.reshape(request_count, spec_rows, kv_heads, grouped, queries.shape[3])
    position = jnp.arange(planes, dtype=jnp.int32) * ctx_count + ctx_index
    allowed = position[None, :] < lengths[:, None]
    scores = jnp.einsum(
        "qskgd,pqkd->qskgp", request_q, key_grid, preferred_element_type=jnp.float32
    )
    weights = weights_of(scores, allowed[:, None, None, None, :])
    numerator = jnp.einsum(
        "qskgp,pqkd->qskgd", weights, value_grid, preferred_element_type=jnp.float32
    )
    denominator = jnp.sum(weights.astype(jnp.float32), axis=-1)
    return (numerator.reshape(queries.shape), denominator.reshape(queries.shape[:3]))


def finish_rows(numerator, denominator, queries, new_keys, new_values, group_index, spec_rows):
    share_rows = numerator.shape[0]
    row_total = new_keys.shape[0]
    query_row = jnp.arange(share_rows, dtype=jnp.int32)
    key_row = jnp.arange(row_total, dtype=jnp.int32)
    earlier = key_row[None, :] <= query_row[:, None]
    same_request = key_row[None, :] // spec_rows == query_row[:, None] // spec_rows
    allowed = jnp.where(group_index == 0, earlier, earlier & same_request)
    scores = jnp.einsum("rkgd,tkd->rkgt", queries, new_keys, preferred_element_type=jnp.float32)
    weights = weights_of(scores, allowed[:, None, None, :])
    numerator = numerator + jnp.einsum(
        "rkgt,tkd->rkgd", weights, new_values, preferred_element_type=jnp.float32
    )
    denominator = denominator + jnp.sum(weights.astype(jnp.float32), axis=-1)
    heads = (numerator / denominator[..., None]).astype(jnp.bfloat16)
    return heads.reshape(share_rows, -1)


def body(
    new_tokens,
    w_query,
    w_key,
    w_value,
    w_out,
    pool_keys,
    pool_values,
    stretch_start,
    lengths,
    dest_blocks,
):
    tokens = new_tokens[0]
    row_total = tokens.shape[0]
    spec_rows = row_total // lengths.shape[0]
    ctx_count = lax.axis_size("ctx")
    ctx_index = lax.axis_index("ctx")
    group_index = lax.axis_index("grp")
    kv_heads = w_key.shape[1] // HD
    grouped = HQ // KVH
    query_sum, key_sum, value_sum = lax.psum(
        (
            jnp.dot(tokens, w_query, preferred_element_type=jnp.float32),
            jnp.dot(tokens, w_key, preferred_element_type=jnp.float32),
            jnp.dot(tokens, w_value, preferred_element_type=jnp.float32),
        ),
        "ctx",
    )
    queries = (query_sum * query_scale).astype(jnp.bfloat16)
    new_keys = key_sum.astype(jnp.bfloat16)
    new_values = value_sum.astype(jnp.bfloat16)
    queries = queries.reshape(row_total, kv_heads, grouped, HD)
    new_keys = new_keys.reshape(row_total, kv_heads, HD)
    new_values = new_values.reshape(row_total, kv_heads, HD)
    pool_k = pool_keys[0]
    pool_v = pool_values[0]
    stretch_first = stretch_start[0]
    slot_count = pool_k.shape[0]

    def prefill_part():
        return prefix_local(queries, pool_k, pool_v, stretch_first, ctx_index * slot_count)

    def decode_part():
        return cache_local(queries, pool_k, pool_v, lengths, ctx_index, ctx_count)

    numerator, denominator = lax.cond(group_index == 0, prefill_part, decode_part)
    numerator, denominator = lax.psum((numerator, denominator), "ctx")
    heads = finish_rows(
        numerator, denominator, queries, new_keys, new_values, group_index, spec_rows
    )
    attn_out = lax.psum_scatter(
        jnp.dot(heads, w_out, preferred_element_type=jnp.float32),
        "tp",
        scatter_dimension=0,
        tiled=True,
    ).astype(jnp.bfloat16)[None]
    got_keys, got_values = passed_along((new_keys, new_values), "grp", 1)
    stored_keys = jnp.where(group_index == 0, new_keys, got_keys)
    stored_values = jnp.where(group_index == 0, new_values, got_values)
    row_ids = jnp.arange(row_total, dtype=jnp.int32)
    landing = jnp.repeat(dest_blocks, BLK) * BLK + row_ids % BLK
    target = jnp.where(group_index == 0, stretch_first + row_ids, landing)
    local_slot = target - ctx_index * slot_count
    local_slot = jnp.where((local_slot >= 0) & (local_slot < slot_count), local_slot, slot_count)
    keys_out = pool_k.at[local_slot].set(stored_keys, mode="drop")[None]
    values_out = pool_v.at[local_slot].set(stored_values, mode="drop")[None]
    return (attn_out, keys_out, values_out)


def solution(mesh):
    return jax.shard_map(
        body,
        mesh=mesh,
        in_specs=(
            P("grp", None, "ctx"),
            P("ctx", "tp"),
            P("ctx", "tp"),
            P("ctx", "tp"),
            P("tp", "ctx"),
            P("grp", "ctx", "tp", None),
            P("grp", "ctx", "tp", None),
            P(),
            P(),
            P(),
        ),
        out_specs=(P("grp", "tp", "ctx"), P("grp", "ctx", "tp", None), P("grp", "ctx", "tp", None)),
        check_vma=False,
    )
```

profile of v0, /device:TPU:64, one launch (start us, length us, event | category | flops | bytes accessed | tf_op | source)
XLA Modules:
  0.0 551.8 jit_solution(12101418127393134708)
XLA Ops:
  7.2 7.8 %copy.161 = bf16[1,5120,4,128]{3,2,1,0:T(4,128)(2,1)} copy(bf16[1,5120,4,128]{3,2,1,0:T(4,128)(2,1)} %param.19) | data formatting | bytes 10485760
  15.0 2.4 copy.162
  17.4 2.1 fusion.23
  19.5 1.5 fusion.19
  21.1 123.0 %all-reduce.5.cloned.1.call-done = f32[512,1024]{1,0:T(8,128)} async-done(((f32[512,1024]{1,0:T(8,128)}), f32[512,1024]{1,0:T(8,128)}) %all-reduce.5.cloned.1.call-update) | async-done | bytes 2097168 | tf_op jit(solution)/shard_map/psum | solution.py:123
  144.0 1.8 multiply_convert_fusion
  145.9 1.6 reshape.241
  147.5 20.1 %conditional.1 = (f32[512,4,2]{0,2,1:T(2,128)}, f32[512,4,2,128]{0,3,2,1:T(8,128)}) conditional(s32[]{:T(128)} %convert_element_type.36, (s32[]{:T(128)}, s32[8]{0:T(128)S(1)}, bf16[1,5120,4,128]{3,2,1,0:T(4,128)(2,1)}, bf16[512,1024]{1,0:T(8,128)(2,1)S(1)}, bf16[1,5120,4,128]{3,2,1,0:T(4,128)(2,1)}) %tuple.71, (bf16[1,5120,4,128]{3,2,1,0:T(4,128)(2,1)}, ...), branch_computations={%region_1.3_spmd, %region_3.7_spmd} | conditional | flops 1357908224 | bytes 50429028 | solution.py:148
  147.5 1.5 reshape_reshape.2
  149.1 10.1 %convert_reduce_fusion = (f32[8,64,4,2]{1,3,2,0:T(2,128)S(1)}, bf16[8,64,4,2,640]{4,1,3,2,0:T(8,128)(2,1)S(1)}) fusion(bf16[8,64,4,2,128]{4,3,2,1,0:T(2,128)(2,1)} %reshape_reshape.2, bf16[640,8,4,128,1]{3,2,1,0,4:T(4,128)(2,1)} %bitcast.93, pred[8,640]{1,0:T(8,128)(4,1)S(1)} %broadcast_compare_fusion), kind=kOutput, calls=%fused_computation.3 | convolution fusion | flops 686813184 | bytes 11555840 | tf_op jit(solution)/shard_map/cond/branch_0_fun/qskgd,pqkd->qskgp/dot_general | solution.py:74
  159.2 5.6 %fusion.7 = f32[8,64,4,2,128]{4,1,3,2,0:T(8,128)S(1)} fusion(bf16[8,64,4,2,640]{4,1,3,2,0:T(8,128)(2,1)S(1)} %get-tuple-element.195, bf16[640,8,4,128,1]{3,2,1,0,4:T(4,128)(2,1)S(1)} %bitcast.99), kind=kOutput, calls=%fused_computation.9 | convolution fusion | flops 671088640 | bytes 12582912 | tf_op jit(solution)/shard_map/cond/branch_0_fun/qskgp,pqkd->qskgd/dot_general | solution.py:78
  165.0 1.9 copy.100
  168.3 70.0 %all-reduce.8 = (bf16[512,512]{1,0:T(8,128)(2,1)S(1)}, f32[512,4,2]{0,2,1:T(2,128)S(1)}, bf16[512,512]{1,0:T(8,128)(2,1)}) all-reduce(f32[512,512]{1,0:T(8,128)} %fusion.19, f32[512,4,2]{0,2,1:T(2,128)} %get-tuple-element.84, f32[512,512]{1,0:T(8,128)S(1)} %fusion.21), channel_id=1, replica_groups=mesh['ctx'=16,'tp'=4,'grp'=2] {'ctx'}, use_global_device_ids=true, to_apply=%region_9.10 | all-reduce | flops 528384 | bytes 3178496 | tf_op jit(solution)/shard_map/psum | solution.py:123
  239.7 4.6 convert_reduce_fusion.2
  244.3 171.0 %all-reduce.7.cloned.1.call-done = f32[512,4,2,128]{0,3,2,1:T(8,128)} async-done(((f32[512,4,2,128]{0,3,2,1:T(8,128)}), f32[512,4,2,128]{0,3,2,1:T(8,128)}) %all-reduce.7.cloned.1.call-update) | async-done | bytes 2097168 | tf_op jit(solution)/shard_map/psum | solution.py:149
  415.2 3.7 fusion.15
  419.0 1.3 fusion.29
  420.3 1.3 collective-permute-start.1
  421.6 1.3 collective-permute-start
  423.7 14.8 %collective-permute-done.1 = bf16[512,4,128]{2,1,0:T(4,128)(2,1)S(1)} collective-permute-done((bf16[512,4,128]{2,1,0:T(4,128)(2,1)S(1)}, bf16[512,4,128]{2,1,0:T(4,128)(2,1)S(1)}, u32[]{:S(2)}, u32[]{:S(2)}) %collective-permute-start.1) | collective-permute-done | bytes 524320 | tf_op jit(solution)/shard_map/ppermute | solution.py:21
  438.5 9.7 %collective-permute-done = bf16[512,4,128]{2,1,0:T(4,128)(2,1)S(1)} collective-permute-done((bf16[512,4,128]{2,1,0:T(4,128)(2,1)S(1)}, bf16[512,4,128]{2,1,0:T(4,128)(2,1)S(1)}, u32[]{:S(2)}, u32[]{:S(2)}) %collective-permute-start) | collective-permute-done | bytes 524320 | tf_op jit(solution)/shard_map/ppermute | solution.py:21
  450.2 46.7 %scatter_fusion.1 = bf16[5120,4,128]{2,1,0:T(4,128)(2,1)} fusion(bf16[5120,4,128]{2,1,0:T(4,128)(2,1)} %bitcast.96, s32[512]{0:T(512)S(1)} %bitcast.112, bf16[512,4,128]{2,1,0:T(4,128)(2,1)S(1)} %bitcast.108), kind=kCustom, calls=%fused_computation.1 | custom fusion | bytes 1574912 | tf_op jit(solution)/shard_map/scatter | solution.py:168
  496.9 46.7 %scatter_fusion = bf16[5120,4,128]{2,1,0:T(4,128)(2,1)} fusion(bf16[5120,4,128]{2,1,0:T(4,128)(2,1)} %bitcast.92, s32[512]{0:T(512)S(1)} %bitcast.113, bf16[512,4,128]{2,1,0:T(4,128)(2,1)S(1)} %bitcast.107), kind=kCustom, calls=%fused_computation | custom fusion | bytes 1574912 | tf_op jit(solution)/shard_map/scatter | solution.py:167
  543.7 1.6 convert_bitcast_fusion
  (48 shorter events, 5.3 us)
Async XLA Ops:
  7.2 10.2 %copy-start = (bf16[288,1024]{1,0:T(8,128)(2,1)S(1)}, bf16[288,1024]{1,0:T(8,128)(2,1)}, u32[]{:S(2)}) copy-start(bf16[288,1024]{1,0:T(8,128)(2,1)} %param.15) | copy-start | bytes 1769476
  7.2 136.9 %all-reduce.5.cloned.1.call-start = ((), (), s32[]{:S(2)}) async-start(), calls=%async_computation.1 | async-start | bytes 4194304 | tf_op jit(solution)/shard_map/psum | solution.py:123
  7.2 7.8 %copy-start.1 = (bf16[1,5120,4,128]{3,2,1,0:T(4,128)(2,1)S(1)}, bf16[1,5120,4,128]{3,2,1,0:T(4,128)(2,1)}, u32[]{:S(2)}) copy-start(bf16[1,5120,4,128]{3,2,1,0:T(4,128)(2,1)} %param.20) | copy-start | bytes 15728644
  15.0 2.4 copy-start.3
  15.0 4.5 copy-start.6
  19.4 128.0 %copy-start.8 = (s32[8]{0:T(128)S(1)}, s32[8]{0:T(128)}, u32[]{:S(2)}) copy-start(s32[8]{0:T(128)} %param.22) | copy-start | bytes 100
  19.5 395.8 %all-reduce.7.cloned.1.call-start = ((), (), s32[]{:S(2)}) async-start(), calls=%async_computation.2 | async-start | bytes 4194304 | tf_op jit(solution)/shard_map/psum | solution.py:149
  147.5 20.2 %copy-start.7 = (bf16[288,512]{1,0:T(8,128)(2,1)S(1)}, bf16[288,512]{1,0:T(8,128)(2,1)}, u32[]{:S(2)}) copy-start(bf16[288,512]{1,0:T(8,128)(2,1)} %param.17) | copy-start | bytes 884740
  147.5 11.7 %slice-start = ((s8[5242880]{0:T(1024)(128)(4,1)}), s8[1048576]{0:T(1024)(128)(4,1)S(1)}, s32[]{:S(2)}) async-start(s8[5242880]{0:T(1024)(128)(4,1)} %bitcast.97), calls=%async_computation.4 | async-start | bytes 2097152 | tf_op jit(solution)/shard_map/cond
  149.1 10.1 %slice-start.1 = ((s8[5242880]{0:T(1024)(128)(4,1)}), s8[4194304]{0:T(1024)(128)(4,1)S(1)}, s32[]{:S(2)}) async-start(s8[5242880]{0:T(1024)(128)(4,1)} %bitcast.97), calls=%async_computation.5 | async-start | bytes 8388608 | tf_op jit(solution)/shard_map/cond
  167.5 72.1 %copy-start.2 = (bf16[512,4,2,128]{3,2,1,0:T(2,128)(2,1)S(1)}, bf16[512,4,2,128]{3,2,1,0:T(2,128)(2,1)}, u32[]{:S(2)}) copy-start(bf16[512,4,2,128]{3,2,1,0:T(2,128)(2,1)} %reshape.241) | copy-start | bytes 3145732
  167.6 376.1 %reduce-scatter.2.cloned.1.call-start = ((), (), s32[]{:S(2)}) async-start(), calls=%async_computation.3 | async-start | bytes 737280 | tf_op jit(solution)/shard_map/reduce_scatter | solution.py:153
  415.2 3.7 copy-start.4
  415.2 8.3 %copy-start.9 = (s32[32]{0:T(128)S(1)}, s32[32]{0:T(128)}, u32[]{:S(2)}) copy-start(s32[32]{0:T(128)} %param.23) | copy-start | bytes 388
  420.3 18.3 %collective-permute-start.1 = (bf16[512,4,128]{2,1,0:T(4,128)(2,1)S(1)}, bf16[512,4,128]{2,1,0:T(4,128)(2,1)S(1)}, u32[]{:S(2)}, u32[]{:S(2)}) collective-permute-start(bf16[512,4,128]{2,1,0:T(4,128)(2,1)S(1)} %reshape.242), channel_id=1, source_target_pairs={{0,1},{2,3},{4,5},{6,7},{8,9},{10,11},{12,13},{14,15},{16,17},{18,... | collective-permute-start | bytes 1572872 | tf_op jit(solution)/shard_map/ppermute | solution.py:21
  421.6 26.7 %collective-permute-start = (bf16[512,4,128]{2,1,0:T(4,128)(2,1)S(1)}, bf16[512,4,128]{2,1,0:T(4,128)(2,1)S(1)}, u32[]{:S(2)}, u32[]{:S(2)}) collective-permute-start(bf16[512,4,128]{2,1,0:T(4,128)(2,1)S(1)} %reshape.243), channel_id=1, source_target_pairs={{0,1},{2,3},{4,5},{6,7},{8,9},{10,11},{12,13},{14,15},{16,17},{18,... | collective-permute-start | bytes 1572872 | tf_op jit(solution)/shard_map/ppermute | solution.py:21
  448.3 0.8 copy-start.5
Sparse Core Ops, SparseCore 0:
  19.6 124.4 all-reduce.4
  167.7 247.5 all-reduce.6
  420.4 22.8 reduce-scatter.1
where the time goes:
time: 555 us; the launch traced here: 552 us
  waiting for transfers between devices  319 us (57%)
  local copies, waits for them, and re-layouts  112 us (20%)
  blocking collectives  70 us (13%)
  matrix products  29.3 us (5%)
  between operations  14.6 us (3%)
    psum x1, waiting for transfers between devices, body(): numerator, denominator = lax.psum((numerator, denominator), 'ctx')  171 us
    psum x1, waiting for transfers between devices, body(): lax.psum((jnp.dot(tokens, w_query, preferred_element_type=jnp.float32), j...  123 us
    psum x1, blocking collectives, body(): lax.psum((jnp.dot(tokens, w_query, preferred_element_type=jnp.float32), j...  70 us
    scatter x1, local copies, waits for them, and re-layouts, body(): keys_out = pool_k.at[local_slot].set(stored_keys, mode='drop')[None]  46.7 us
    scatter x1, local copies, waits for them, and re-layouts, body(): values_out = pool_v.at[local_slot].set(stored_values, mode='drop')[None]  46.7 us
    ppermute x2, waiting for transfers between devices, passed_along(): lax.ppermute(value, axis, [(source, source + steps) for source in range(l...  24.5 us
  transfers between devices with their start and end apart: 5, of which 4 were waited for; matrix products, arithmetic and copies ran while one was open for 19% of the time, Pallas kernels for 0%

commit v1 on v0

v1 whole, which is shorter than its diff:
```python
import jax
import jax.numpy as jnp
from jax import lax
from jax.experimental import pallas as pl
from jax.experimental.pallas import tpu as pltpu
from jax.sharding import PartitionSpec as P

HD = 128
GROUPED = 2
BLK = 16
REQS = 8
ROWS = 512
SLOTS_DEV = 5120
HEADS = 4
CHIPS = 8
SHARE = 32
UNIT = GROUPED * SHARE
MSG = UNIT + 16
DEINT = 512
CHUNK = 1024
STEPS = SLOTS_DEV // CHUNK
MODEL = 288
LOG2E = 1.4426950408889634

soft_cap = 50.0
query_scale = 1.0 / 12.0
bf16 = jnp.bfloat16
f32 = jnp.float32


def weights_of(scores):
    return jnp.exp2(jnp.tanh(scores * (1.0 / soft_cap)) * (soft_cap * LOG2E))


def pack_den(den):
    high = den.astype(bf16)
    low = (den - high.astype(f32)).astype(bf16)
    return jnp.concatenate([high, low], axis=-2)


def layer_kernel(
    start_ref, len_ref, tok_ref, wq_ref, wk_ref, wv_ref, wo_ref, pool_k, pool_v,
    out_ref, kv_out,
    kbuf, vbuf, kfl, vfl, kh, vh, acc,
    st1, cx1, sn1, rs1, qfull, kvown, kvgot, kvfull, kself, vself, kvfl,
    st3, cx3, sn3, rs3, hfull, oacc, st5, rs5,
    in_sem, out_sem, cx1_s, cx1_r, rs1_s, rs1_r, ag_s, ag_r, fw_s, fw_r, gr_s, gr_r,
    cx3_s, cx3_r, rs3_s, rs3_r, p5_s, p5_r,
):
    ctx = lax.axis_index("ctx")
    tp = lax.axis_index("tp")
    grp = lax.axis_index("grp")
    chip = ctx // 2
    core = lax.rem(ctx, 2)
    other = 1 - core
    sibling = {"ctx": 2 * chip + other}
    twin = {"grp": 1 - grp}

    def peer(d):
        return lax.rem(chip + d, CHIPS)

    def on_chip(k):
        return {"ctx": 2 * k + core}

    def remote(src, dst, send, recv, device):
        return pltpu.make_async_remote_copy(
            src_ref=src, dst_ref=dst, send_sem=send, recv_sem=recv, device_id=device,
            device_id_type=pl.DeviceIdType.MESH,
        )

    rows = DEINT * HEADS
    parts = SLOTS_DEV // DEINT

    def pool_in(j, which):
        src, dst = ((pool_k, kbuf), (pool_v, vbuf))[which]
        at = pl.ds(pl.multiple_of(j * rows, rows), rows)
        return pltpu.make_async_copy(src.at[at], dst.at[at], in_sem.at[which, j])

    @pl.loop(0, parts)
    def _(j):
        pool_in(j, 0).start()
        pool_in(j, 1).start()

    barrier = pltpu.get_barrier_semaphore()

    def greet(device):
        pl.semaphore_signal(barrier, inc=1, device_id=device, device_id_type=pl.DeviceIdType.MESH)

    greet(sibling)
    greet(twin)
    for d in range(1, CHIPS):
        greet(on_chip(peer(d)))
    for d in range(1, 4):
        greet({"tp": lax.rem(tp + d, 4)})
    pl.semaphore_wait(barrier, 2 + CHIPS - 1 + 3)

    def cx1_copy(u):
        return remote(st1.at[u, other], cx1.at[u], cx1_s.at[u], cx1_r.at[u], sibling)

    def rs1_send(u, k):
        return remote(sn1.at[u, k], rs1.at[u, chip], rs1_s.at[u, k], rs1_r.at[u, chip], on_chip(k))

    def rs1_recv(u, k):
        return remote(rs1.at[u, k], rs1.at[u, k], rs1_s.at[u, k], rs1_r.at[u, k], on_chip(k))

    def full_at(u, k, p):
        return qfull.at[u, k, p]

    def ag_send(ref, u, k):
        return remote(ref.at[chip, core], ref.at[chip, core], ag_s.at[u, k], ag_r.at[u, chip], on_chip(k))

    def ag_recv(ref, u, k):
        return remote(ref.at[k, core], ref.at[k, core], ag_s.at[u, k], ag_r.at[u, k], on_chip(k))

    def fw_send(ref, u, k):
        return remote(ref.at[k, core], ref.at[k, core], fw_s.at[u, k], fw_r.at[u, k], sibling)

    def fw_recv(ref, u, k):
        return remote(ref.at[k, other], ref.at[k, other], fw_s.at[u, k], fw_r.at[u, k], sibling)

    def share_out(ref, u):
        for d in range(1, CHIPS):
            ag_send(ref, u, peer(d)).start()
        fw_send(ref, u, chip).start()

    def forward(ref, u):
        @pl.loop(1, CHIPS)
        def _(d):
            k = peer(d)
            ag_recv(ref, u, k).wait_recv()
            fw_send(ref, u, k).start()

    def gathered(ref, u):
        @pl.loop(0, CHIPS)
        def _(k):
            fw_recv(ref, u, k).wait_recv()

    def shared_done(ref, u):
        @pl.loop(1, CHIPS)
        def _(d):
            ag_send(ref, u, peer(d)).wait_send()

        @pl.loop(0, CHIPS)
        def _(k):
            fw_send(ref, u, k).wait_send()

    sources = [(wq_ref, h * 256) for h in range(4)] + [
        (wk_ref, 0), (wk_ref, 256), (wv_ref, 0), (wv_ref, 256)]
    for u, (w, at) in enumerate(sources):
        part = lax.dot_general(
            tok_ref[...], w[:, at:at + 256], (((0,), (0,)), ((), ())), preferred_element_type=f32
        ).astype(bf16)
        for g in range(2):
            piece = part[:, g * HD:(g + 1) * HD].reshape(CHIPS, 2, SHARE, HD)
            for p in range(2):
                st1[u, p, :, g * SHARE:(g + 1) * SHARE, :] = piece[:, p]
        cx1_copy(u).start()

    def reduce_cores(u):
        cx1_copy(u).wait_recv()
        both = (st1[u, core].astype(f32) + cx1[u].astype(f32)).astype(bf16)
        sn1[u] = both
        rs1[u, chip] = sn1[u, chip]
        for d in range(1, CHIPS):
            rs1_send(u, peer(d)).start()

    def total1(u):
        @pl.loop(1, CHIPS)
        def _(d):
            rs1_recv(u, peer(d)).wait_recv()

        total = rs1[u, 0].astype(f32)
        for k in range(1, CHIPS):
            total = total + rs1[u, k].astype(f32)
        return total

    def finish_query(u):
        qfull[u, chip, core] = (total1(u) * query_scale).astype(bf16)
        share_out(qfull.at[u], u)

    lane_row = lax.broadcasted_iota(jnp.int32, (REQS, HD), 0)
    limits = jnp.zeros((REQS, HD), jnp.int32)
    for r in range(REQS):
        limits = jnp.where(lane_row == r, len_ref[r], limits)
    limits = jnp.where(grp == 0, start_ref[0], limits)

    def deint(j):
        pool_in(j, 0).wait()
        pool_in(j, 1).wait()
        at = pl.ds(pl.multiple_of(j * rows, rows), rows)
        kfl[...] = kbuf[at].astype(f32)
        vfl[...] = vbuf[at].astype(f32)
        slot = j * DEINT + lax.broadcasted_iota(jnp.int32, (DEINT // REQS, REQS, HD), 0) * REQS \
            + lax.broadcasted_iota(jnp.int32, (DEINT // REQS, REQS, HD), 1)
        position = jnp.where(grp == 0, ctx * SLOTS_DEV + slot, ctx + 16 * (slot // REQS))
        seen = (position < limits[None]).reshape(DEINT, HD)
        ones = jnp.where(seen, 1.0, 0.0).astype(bf16)
        to = pl.ds(pl.multiple_of(j * DEINT, DEINT), DEINT)
        for h in range(HEADS):
            kh[h, to, :] = kfl[pl.ds(h, DEINT, stride=HEADS)].astype(bf16)
            vh[h, to, 0:HD] = jnp.where(seen, vfl[pl.ds(h, DEINT, stride=HEADS)], 0.0).astype(bf16)
            vh[h, to, HD:2 * HD] = ones

    def deint_range(first, last):
        @pl.loop(first, last)
        def _(j):
            deint(j)

    deint_range(0, 2)
    for u in range(4):
        reduce_cores(u)
    deint_range(2, 5)
    finish_query(0)
    finish_query(1)
    deint_range(5, 7)
    finish_query(2)
    finish_query(3)
    for u in range(4, 8):
        reduce_cores(u)
    forward(qfull.at[0], 0)
    deint_range(7, parts)
    acc[...] = jnp.zeros_like(acc)
    kself[...] = jnp.zeros_like(kself)
    vself[...] = jnp.zeros_like(vself)
    gathered(qfull.at[0], 0)

    def queries_of(h):
        return qfull[h].reshape(ROWS * GROUPED, HD)

    def rowkeys(width):
        row = lax.broadcasted_iota(jnp.int32, (ROWS * GROUPED, width), 0)
        return jnp.where(grp == 0, 0, row // (2 * UNIT))

    def attend(h, j):
        at = pl.ds(pl.multiple_of(j * CHUNK, CHUNK), CHUNK)
        scores = lax.dot_general(
            queries_of(h), kh[h, at, :], (((1,), (1,)), ((), ())), preferred_element_type=f32
        )
        column = lax.broadcasted_iota(jnp.int32, (ROWS * GROUPED, CHUNK), 1)
        slotkey = jnp.where(grp == 0, 0, lax.rem(column, REQS))
        weights = jnp.where(rowkeys(CHUNK) == slotkey, weights_of(scores), 0.0).astype(bf16)
        acc[h] += jnp.dot(weights, vh[h, at, :], preferred_element_type=f32)

    def attend_self(h):
        scores = lax.dot_general(
            queries_of(h), kself[h], (((1,), (1,)), ((), ())), preferred_element_type=f32
        )
        index = lax.broadcasted_iota(jnp.int32, (ROWS * GROUPED, HD), 0)
        row = SHARE * (index // UNIT) + lax.rem(index, SHARE)
        key = SHARE * ctx + lax.broadcasted_iota(jnp.int32, (ROWS * GROUPED, HD), 1)
        mine = jnp.where(grp == 0, 0, ctx // 2)
        allowed = (key <= row) & (rowkeys(HD) == mine)
        weights = jnp.where(allowed, weights_of(scores), 0.0).astype(bf16)
        acc[h] += jnp.dot(weights, vself[h], preferred_element_type=f32)

    def cx3_copy(h):
        return remote(st3.at[h, other], cx3.at[h], cx3_s.at[h], cx3_r.at[h], sibling)

    def rs3_send(h, k):
        return remote(sn3.at[h, k], rs3.at[h, chip], rs3_s.at[h, k], rs3_r.at[h, chip], on_chip(k))

    def rs3_recv(h, k):
        return remote(rs3.at[h, k], rs3.at[h, k], rs3_s.at[h, k], rs3_r.at[h, k], on_chip(k))

    lane8 = lax.broadcasted_iota(jnp.int32, (2 * CHIPS, 8, HD), 2) // 16

    def hand_over(h):
        num = acc[h, :, 0:HD].astype(bf16).reshape(CHIPS, 2, UNIT, HD)
        den = acc[h, :, HD:2 * HD].reshape(2 * CHIPS, 8, 8, HD)
        small = den[:, 0]
        for a in range(1, 8):
            small = jnp.where(lane8 == a, den[:, a], small)
        small = pack_den(small).reshape(CHIPS, 2, 16, HD)
        for p in range(2):
            st3[h, p, :, 0:UNIT, :] = num[:, p]
            st3[h, p, :, UNIT:MSG, :] = small[:, p]
        cx3_copy(h).start()

    def den_of(block):
        return block[:, UNIT:UNIT + 8].astype(f32) + block[:, UNIT + 8:MSG].astype(f32)

    def reduce_cores3(h):
        cx3_copy(h).wait_recv()
        mine = st3[h, core]
        got = cx3[h]
        sn3[h, :, 0:UNIT, :] = (mine[:, 0:UNIT].astype(f32) + got[:, 0:UNIT].astype(f32)).astype(bf16)
        sn3[h, :, UNIT:MSG, :] = pack_den(den_of(mine) + den_of(got))
        rs3[h, chip] = sn3[h, chip]
        for d in range(1, CHIPS):
            rs3_send(h, peer(d)).start()

    def finish_heads(h):
        @pl.loop(1, CHIPS)
        def _(d):
            rs3_recv(h, peer(d)).wait_recv()

        got = rs3[h]
        num = jnp.sum(got[:, 0:UNIT].astype(f32), axis=0)
        den = jnp.sum(den_of(got), axis=0)
        wide = jnp.concatenate(
            [jnp.broadcast_to(den[:, 16 * a:16 * a + 1], (8, HD)) for a in range(8)], axis=0)
        hfull[h, chip, core] = (num / wide).astype(bf16)
        share_out(hfull.at[h], h + 5)

    def finish_kv():
        for u in range(4, 8):
            total = total1(u).astype(bf16)
            for half in range(2):
                h = 2 * (u % 2) + half
                piece = total[half * SHARE:(half + 1) * SHARE]
                if u < 6:
                    kself[h, 0:SHARE, :] = piece
                    kvfl[0, pl.ds(h, SHARE, stride=HEADS), :] = piece.astype(f32)
                else:
                    vself[h, 0:SHARE, 0:HD] = piece
                    vself[h, 0:SHARE, HD:2 * HD] = jnp.ones((SHARE, HD), bf16)
                    kvfl[1, pl.ds(h, SHARE, stride=HEADS), :] = piece.astype(f32)
        kvown[...] = kvfl[...].astype(bf16)
        remote(kvown, kvgot, gr_s, gr_r, twin).start()

    def share_kv():
        remote(kvown, kvgot, gr_s, gr_r, twin).wait_recv()
        kvfull[chip, core] = jnp.where(grp == 0, kvown[...].astype(f32), kvgot[...].astype(f32)).astype(bf16)
        share_out(kvfull, 4)

    kv_store = pltpu.make_async_copy(kvfull, kv_out, out_sem)

    @pl.loop(0, HEADS * STEPS)
    def _(it):
        h = it // STEPS
        j = lax.rem(it, STEPS)

        @pl.when((h == 0) & (j >= 1) & (j <= 3))
        def _():
            forward(qfull.at[j], j)

        @pl.when((h == 0) & (j == 4))
        def _():
            finish_kv()

        @pl.when((h >= 1) & (j == 0))
        def _():
            gathered(qfull.at[h], h)

        @pl.when((h >= 1) & (j == 1))
        def _():
            reduce_cores3(h - 1)

        @pl.when((h >= 1) & (j == 3))
        def _():
            finish_heads(h - 1)

        @pl.when((h >= 1) & (j == 4))
        def _():
            forward(hfull.at[h - 1], h + 4)

        @pl.when((h == 1) & (j == 2))
        def _():
            share_kv()

        @pl.when((h == 2) & (j == 2))
        def _():
            forward(kvfull, 4)

        @pl.when((h == 3) & (j == 2))
        def _():
            gathered(kvfull, 4)
            kv_store.start()

        attend(h, j)

        @pl.when(j == STEPS - 1)
        def _():
            attend_self(h)
            hand_over(h)

    def project(h):
        heads = hfull[h].reshape(2 * CHIPS, 2, SHARE, HD)
        lhs = jnp.concatenate([heads[:, 0].reshape(ROWS, HD), heads[:, 1].reshape(ROWS, HD)], axis=1)
        return lax.dot_general(
            lhs, wo_ref[:, h * 256:(h + 1) * 256], (((1,), (1,)), ((), ())), preferred_element_type=f32
        )

    reduce_cores3(HEADS - 1)
    for h in range(HEADS - 1):
        gathered(hfull.at[h], h + 5)
    total = project(0) + project(1) + project(2)
    oacc[...] = total
    finish_heads(HEADS - 1)
    forward(hfull.at[HEADS - 1], HEADS + 4)
    gathered(hfull.at[HEADS - 1], HEADS + 4)
    oacc[...] += project(HEADS - 1)
    st5[...] = oacc[...].astype(bf16).reshape(4, ROWS // 4, MODEL)

    def p5_copy(d):
        to = lax.rem(tp + d, 4)
        return remote(st5.at[to], rs5.at[d - 1], p5_s.at[d - 1], p5_r.at[d - 1], {"tp": to})

    for d in range(1, 4):
        p5_copy(d).start()
    own = oacc[pl.ds(pl.multiple_of(tp * (ROWS // 4), ROWS // 4), ROWS // 4), :]
    for d in range(1, 4):
        p5_copy(d).wait_recv()
        own = own + rs5[d - 1].astype(f32)
    out_ref[...] = own.astype(bf16)

    @pl.loop(0, 8)
    def _(u):
        cx1_copy(u).wait_send()

        @pl.loop(1, CHIPS)
        def _(d):
            rs1_send(u, peer(d)).wait_send()

    @pl.loop(0, HEADS)
    def _(h):
        cx3_copy(h).wait_send()
        shared_done(qfull.at[h], h)
        shared_done(hfull.at[h], h + 5)

        @pl.loop(1, CHIPS)
        def _(d):
            rs3_send(h, peer(d)).wait_send()

    shared_done(kvfull, 4)
    remote(kvown, kvgot, gr_s, gr_r, twin).wait_send()
    for d in range(1, 4):
        p5_copy(d).wait_send()
    kv_store.wait()


def layer(start, lengths, tok, wq, wk, wv, wo, pool_k, pool_v):
    vmem, dma = pltpu.VMEM, pltpu.SemaphoreType.DMA
    inside = pl.BlockSpec(memory_space=pltpu.VMEM)
    outside = pl.BlockSpec(memory_space=pl.ANY)
    small = pl.BlockSpec(memory_space=pltpu.SMEM)
    share = (2 * HEADS, CHIPS, UNIT, HD)
    msg = (HEADS, CHIPS, MSG, HD)
    return pl.pallas_call(
        layer_kernel,
        name="layer",
        out_shape=(
            jax.ShapeDtypeStruct((ROWS // 4, MODEL), bf16),
            jax.ShapeDtypeStruct((CHIPS, 2, 2, SHARE * HEADS, HD), bf16),
        ),
        in_specs=[small, small] + [inside] * 5 + [outside] * 2,
        out_specs=(inside, outside),
        scratch_shapes=[
            vmem((SLOTS_DEV * HEADS, HD), bf16),
            vmem((SLOTS_DEV * HEADS, HD), bf16),
            vmem((DEINT * HEADS, HD), f32),
            vmem((DEINT * HEADS, HD), f32),
            vmem((HEADS, SLOTS_DEV, HD), bf16),
            vmem((HEADS, SLOTS_DEV, 2 * HD), bf16),
            vmem((HEADS, ROWS * GROUPED, 2 * HD), f32),
            vmem((2 * HEADS, 2, CHIPS, UNIT, HD), bf16),
            vmem(share, bf16),
            vmem(share, bf16),
            vmem(share, bf16),
            vmem((HEADS, CHIPS, 2, UNIT, HD), bf16),
            vmem((2, SHARE * HEADS, HD), bf16),
            vmem((2, SHARE * HEADS, HD), bf16),
            vmem((CHIPS, 2, 2, SHARE * HEADS, HD), bf16),
            vmem((HEADS, HD, HD), bf16),
            vmem((HEADS, HD, 2 * HD), bf16),
            vmem((2, SHARE * HEADS, HD), f32),
            vmem((HEADS, 2, CHIPS, MSG, HD), bf16),
            vmem(msg, bf16),
            vmem(msg, bf16),
            vmem(msg, bf16),
            vmem((HEADS, CHIPS, 2, UNIT, HD), bf16),
            vmem((ROWS, MODEL), f32),
            vmem((4, ROWS // 4, MODEL), bf16),
            vmem((3, ROWS // 4, MODEL), bf16),
            dma((2, SLOTS_DEV // DEINT)),
            dma(()),
            dma((8,)), dma((8,)),
            dma((8, CHIPS)), dma((8, CHIPS)),
            dma((9, CHIPS)), dma((9, CHIPS)),
            dma((9, CHIPS)), dma((9, CHIPS)),
            dma(()), dma(()),
            dma((HEADS,)), dma((HEADS,)),
            dma((HEADS, CHIPS)), dma((HEADS, CHIPS)),
            dma((3,)), dma((3,)),
        ],
        compiler_params=pltpu.CompilerParams(
            collective_id=0, has_side_effects=True, vmem_limit_bytes=60 * 2**20),
        cost_estimate=pl.CostEstimate(
            flops=22 * 10**9, bytes_accessed=14 * 2**20, transcendentals=42 * 10**6),
    )(start, lengths, tok, wq, wk, wv, wo, pool_k, pool_v)


COPIES = 8


def store_kernel(where_ref, first_ref, kv, pool_k, pool_v, keys_out, values_out, copy_sem, row_sem):
    span = SLOTS_DEV // COPIES

    def whole(which, i):
        src, dst = ((pool_k, keys_out), (pool_v, values_out))[which]
        return pltpu.make_async_copy(
            src.at[pl.ds(i * span, span)], dst.at[pl.ds(i * span, span)], copy_sem.at[which, i])

    for i in range(COPIES):
        for which in range(2):
            whole(which, i).start()
    for i in range(COPIES):
        for which in range(2):
            whole(which, i).wait()

    def block(b, which):
        dst = (keys_out, values_out)[which]
        return pltpu.make_async_copy(
            kv.at[b // 4, lax.rem(b // 2, 2), which, pl.ds(lax.rem(b, 2) * BLK, BLK)],
            dst.at[pl.ds(where_ref[b] - first_ref[0], BLK)], row_sem.at[which, b])

    def inside(b):
        at = where_ref[b] - first_ref[0]
        return (at >= 0) & (at <= SLOTS_DEV - BLK)

    def across(b):
        at = where_ref[b] - first_ref[0]
        return ((at > -BLK) & (at < 0)) | ((at > SLOTS_DEV - BLK) & (at < SLOTS_DEV))

    blocks = ROWS // BLK

    @pl.loop(0, blocks)
    def _(b):
        @pl.when(inside(b))
        def _():
            block(b, 0).start()
            block(b, 1).start()

        @pl.when(across(b))
        def _():
            @pl.loop(0, BLK)
            def _(i):
                at = where_ref[b] - first_ref[0] + i

                @pl.when((at >= 0) & (at < SLOTS_DEV))
                def _():
                    for which in range(2):
                        row = pltpu.make_async_copy(
                            kv.at[b // 4, lax.rem(b // 2, 2), which,
                                  pl.ds(lax.rem(b, 2) * BLK + i, 1)],
                            (keys_out, values_out)[which].at[pl.ds(at, 1)],
                            row_sem.at[which, b])
                        row.start()
                        row.wait()

    @pl.loop(0, blocks)
    def _(b):
        @pl.when(inside(b))
        def _():
            block(b, 0).wait()
            block(b, 1).wait()


def store(where, first, kv, pool_k, pool_v):
    dma = pltpu.SemaphoreType.DMA
    outside = pl.BlockSpec(memory_space=pl.ANY)
    small = pl.BlockSpec(memory_space=pltpu.SMEM)
    shape = jax.ShapeDtypeStruct((SLOTS_DEV, HEADS, HD), bf16)
    return pl.pallas_call(
        store_kernel,
        name="store",
        out_shape=(shape, shape),
        in_specs=[small, small] + [outside] * 3,
        out_specs=(outside, outside),
        scratch_shapes=[dma((2, COPIES)), dma((2, ROWS // BLK))],
        cost_estimate=pl.CostEstimate(flops=0, bytes_accessed=21 * 2**20, transcendentals=0),
    )(where, first, kv, pool_k, pool_v)


def body(
    new_tokens, w_query, w_key, w_value, w_out, pool_keys, pool_values, stretch_start, lengths, dest_blocks
):
    flat = (SLOTS_DEV * HEADS, HD)
    pool_k = pool_keys.reshape(flat)
    pool_v = pool_values.reshape(flat)
    out, kv = layer(
        stretch_start, lengths, new_tokens[0].T, w_query, w_key, w_value, w_out.T, pool_k, pool_v)
    blocks = jnp.arange(ROWS // BLK, dtype=jnp.int32) * BLK
    where = jnp.where(lax.axis_index("grp") == 0, stretch_start[0] + blocks, dest_blocks * BLK)
    first = (lax.axis_index("ctx") * SLOTS_DEV).astype(jnp.int32).reshape(1)
    kv = kv.reshape(CHIPS, 2, 2, SHARE, HEADS, HD)
    keys_out, values_out = store(where, first, kv, pool_keys[0], pool_values[0])
    return out[None], keys_out[None], values_out[None]


def solution(mesh):
    return jax.shard_map(
        body,
        mesh=mesh,
        in_specs=(
            P("grp", None, "ctx"),
            P("ctx", "tp"),
            P("ctx", "tp"),
            P("ctx", "tp"),
            P("tp", "ctx"),
            P("grp", "ctx", "tp", None),
            P("grp", "ctx", "tp", None),
            P(),
            P(),
            P(),
        ),
        out_specs=(P("grp", "tp", "ctx"), P("grp", "ctx", "tp", None), P("grp", "ctx", "tp", None)),
        check_vma=False,
    )
```

time: 555 us -> 456 us (0.82)
  the two profiles are of different devices: /device:TPU:64 before, /device:TPU:56 now
where the time goes in v1:
time: 456 us
  Pallas kernels  451 us (99%)
    pallas_call x1, Pallas kernels, store(): pl.pallas_call(store_kernel, name='store', out_shape=(shape, shape), in_s...  353 us
    pallas_call x1, Pallas kernels, layer(): pl.pallas_call(layer_kernel, name='layer', out_shape=(jax.ShapeDtypeStruc...  98.5 us

profile of v1, /device:TPU:56, one launch (start us, length us, event | category | flops | bytes accessed | tf_op | source)
XLA Modules:
  0.0 455.6 jit_solution(12751004005844619702)
XLA Ops:
  1.3 1.2 broadcast_select_fusion.where_ref
  2.5 98.5 %layer.1 = (bf16[128,288]{1,0:T(8,128)(2,1)}, bf16[8,2,2,128,128]{4,3,2,1,0:T(8,128)(2,1)}) custom-call(s32[1]{0:T(128)} %copy.14.start_ref, s32[8]{0:T(128)} %len_ref.1, bf16[288,512]{1,0:T(8,128)(2,1)} %bitcast.24, bf16[288,1024]{1,0:T(8,128)(2,1)} %wq_ref.1, bf16[288,512]{1,0:T(8,128)(2,1)} %wk_ref.1, bf16[288,512]{1,0:T(8,128)(2,1)} %wv_ref.1, ...), custom_call_target="tpu_custom_call" | custom-call | flops 22000001024 | bytes 14680064 | tf_op jit(solution)/shard_map/layer/pallas_call | solution.py:439
  101.0 1.6 copy.13
  102.6 353.0 %store.1 = (bf16[5120,4,128]{2,1,0:T(4,128)(2,1)}, bf16[5120,4,128]{2,1,0:T(4,128)(2,1)}) custom-call(s32[32]{0:T(128)} %broadcast_select_fusion.where_ref, s32[1]{0:T(128)} %bitcast.7.first_ref, bf16[8,2,2,32,4,128]{5,4,3,2,1,0:T(4,128)(2,1)} %bitcast.19, bf16[5120,4,128]{2,1,0:T(4,128)(2,1)} %bitcast.16, bf16[5120,4,128]{2,1,0:T(4,128)(2,1)} %bitcast.18), custom_call_target="tpu_custom_call" | custom-call | bytes 22020096 | tf_op jit(solution)/shard_map/store/pallas_call | solution.py:564

commit v2 on v1

v2 whole, which is shorter than its diff:
```python
import jax
import jax.numpy as jnp
from jax import lax
from jax.experimental import pallas as pl
from jax.experimental.pallas import tpu as pltpu
from jax.sharding import PartitionSpec as P

HD = 128
GROUPED = 2
BLK = 16
REQS = 8
ROWS = 512
SLOTS_DEV = 5120
HEADS = 4
CHIPS = 8
SHARE = 32
UNIT = GROUPED * SHARE
MSG = UNIT + 16
DEINT = 512
PIECE = 128
CHUNK = 1280
CHUNKS = 2
STEPS = SLOTS_DEV // (CHUNK * CHUNKS)
MODEL = 288
LOG2E = 1.4426950408889634

soft_cap = 50.0
query_scale = 1.0 / 12.0
bf16 = jnp.bfloat16
f32 = jnp.float32


def weights_of(scores):
    return jnp.exp2(jnp.tanh(scores * (1.0 / soft_cap)) * (soft_cap * LOG2E))


def pack_den(den):
    high = den.astype(bf16)
    low = (den - high.astype(f32)).astype(bf16)
    return jnp.concatenate([high, low], axis=-2)


def layer_kernel(
    start_ref, len_ref, tok_ref, wq_ref, wk_ref, wv_ref, wo_ref, pool_k, pool_v,
    out_ref, kv_out,
    kbuf, vbuf, kfl, vfl, kh, vh, ones, acc, meets,
    st1, cx1, sn1, rs1, qfull, kvown, kvgot, kvfull, kself, vself, kvfl,
    st3, cx3, sn3, rs3, hfull, wo_got, oacc, st5, rs5,
    in_sem, out_sem, cx1_s, cx1_r, rs1_s, rs1_r, agq_s, agq_r, fwq_s, fwq_r, agk_s, agk_r, fwk_s, fwk_r,
    agh_s, agh_r, gr_s, gr_r, wo_s, wo_r,
    cx3_s, cx3_r, rs3_s, rs3_r, p5_s, p5_r,
):
    ctx = lax.axis_index("ctx")
    tp = lax.axis_index("tp")
    grp = lax.axis_index("grp")
    chip = ctx // 2
    core = lax.rem(ctx, 2)
    other = 1 - core
    sibling = {"ctx": 2 * chip + other}
    twin = {"grp": 1 - grp}

    def peer(d):
        return lax.rem(chip + d, CHIPS)

    def on_chip(k):
        return {"ctx": 2 * k + core}

    def remote(src, dst, send, recv, device):
        return pltpu.make_async_remote_copy(
            src_ref=src, dst_ref=dst, send_sem=send, recv_sem=recv, device_id=device,
            device_id_type=pl.DeviceIdType.MESH,
        )

    rows = DEINT * HEADS
    parts = SLOTS_DEV // DEINT

    def pool_in(j, which):
        src, dst = ((pool_k, kbuf), (pool_v, vbuf))[which]
        at = pl.ds(pl.multiple_of(j * rows, rows), rows)
        return pltpu.make_async_copy(src.at[at], dst.at[at], in_sem.at[which, j])

    @pl.loop(0, parts)
    def _(j):
        pool_in(j, 0).start()
        pool_in(j, 1).start()

    barrier = pltpu.get_barrier_semaphore()

    def greet(device):
        pl.semaphore_signal(barrier, inc=1, device_id=device, device_id_type=pl.DeviceIdType.MESH)

    greet(sibling)
    greet(twin)
    for d in range(1, CHIPS):
        greet(on_chip(peer(d)))
    for d in range(1, 4):
        greet({"tp": lax.rem(tp + d, 4)})
        greet({"ctx": 2 * chip + other, "tp": lax.rem(tp + d, 4)})

    def cx1_copy(u):
        return remote(st1.at[u, other], cx1.at[u], cx1_s.at[u], cx1_r.at[u], sibling)

    seven = pl.ds(0, CHIPS - 1)

    def rs1_send(u, k):
        return remote(sn1.at[u, k], rs1.at[u, chip], rs1_s, rs1_r.at[u], on_chip(k))

    def rs1_all(u):
        return remote(sn1.at[u, seven], rs1.at[u, seven], rs1_s, rs1_r.at[u], sibling)

    def ag_send(buf, u, k):
        ref, send, recv, _, _ = buf
        return remote(ref.at[u, chip, core], ref.at[u, chip, core], send, recv.at[u], on_chip(k))

    def ag_all(buf, u):
        ref, send, recv, _, _ = buf
        return remote(ref.at[u, seven, core], ref.at[u, seven, core], send, recv.at[u], sibling)

    def fw_send(buf, u):
        ref, _, _, send, recv = buf
        return remote(ref.at[u, :, core], ref.at[u, :, core], send.at[u], recv.at[u], sibling)

    def share_out(buf, u):
        for d in range(1, CHIPS):
            ag_send(buf, u, peer(d)).start()

    def forward(buf, u):
        ag_all(buf, u).wait_recv()
        fw_send(buf, u).start()

    def gathered(buf, u):
        ref, _, _, send, recv = buf
        remote(ref.at[u, :, other], ref.at[u, :, other], send.at[u], recv.at[u], sibling).wait_recv()

    def shared_done(buf, u):
        ag_all(buf, u).wait_send()
        fw_send(buf, u).wait_send()

    queries = (qfull, agq_s, agq_r, fwq_s, fwq_r)
    new_rows = (kvfull, agk_s, agk_r, fwk_s, fwk_r)
    heads_out = (hfull, agh_s, agh_r, None, None)

    wo_copy = remote(wo_ref, wo_got, wo_s, wo_r, sibling)

    def project_in(w_ref, first):
        part = lax.dot_general(
            tok_ref[...], w_ref[...], (((0,), (0,)), ((), ())), preferred_element_type=f32
        ).astype(bf16)
        for n in range(part.shape[1] // HD):
            piece = part[:, n * HD:(n + 1) * HD].reshape(CHIPS, 2, SHARE, HD)
            u, g = first + n // 2, n % 2
            for p in range(2):
                st1[u, p, :, g * SHARE:(g + 1) * SHARE, :] = piece[:, p]

    project_in(wq_ref, 0)
    pl.semaphore_wait(barrier, 2 + CHIPS - 1 + 6)
    for u in range(4):
        cx1_copy(u).start()
    project_in(wk_ref, 4)
    project_in(wv_ref, 6)
    for u in range(4, 8):
        cx1_copy(u).start()
    wo_copy.start()

    def reduce_cores(u):
        cx1_copy(u).wait_recv()
        both = (st1[u, core].astype(f32) + cx1[u].astype(f32)).astype(bf16)
        sn1[u] = both
        rs1[u, chip] = sn1[u, chip]
        for d in range(1, CHIPS):
            rs1_send(u, peer(d)).start()

    def total1(u):
        rs1_all(u).wait_recv()
        total = rs1[u, 0].astype(f32)
        for k in range(1, CHIPS):
            total = total + rs1[u, k].astype(f32)
        return total

    def finish_query(u):
        qfull[u, chip, core] = (total1(u) * query_scale).astype(bf16)
        share_out(queries, u)

    lane_row = lax.broadcasted_iota(jnp.int32, (REQS, HD), 0)
    limits = jnp.zeros((REQS, HD), jnp.int32)
    for r in range(REQS):
        limits = jnp.where(lane_row == r, len_ref[r], limits)
    limits = jnp.where(grp == 0, start_ref[0] - ctx * SLOTS_DEV - lane_row, limits - ctx)
    plane_step = jnp.where(grp == 0, REQS, 16)
    piece_planes = PIECE // REQS
    plane_of = lax.broadcasted_iota(jnp.int32, (piece_planes, REQS, HD), 0) * plane_step

    def deint(j):
        pool_in(j, 0).wait()
        pool_in(j, 1).wait()

        @pl.loop(0, DEINT // PIECE)
        def _(i):
            first = j * DEINT + i * PIECE
            at = pl.ds(pl.multiple_of(first * HEADS, PIECE * HEADS), PIECE * HEADS)
            to = pl.ds(pl.multiple_of(first, PIECE), PIECE)
            kfl[...] = kbuf[at].astype(f32)
            vfl[...] = vbuf[at].astype(f32)
            planes = plane_of + (first // REQS) * plane_step
            seen = jnp.where(planes < limits[None], 1.0, 0.0).reshape(PIECE, HD)
            ones[to, :] = seen.astype(bf16)
            for h in range(HEADS):
                kh[h, to, :] = kfl[pl.ds(h, PIECE, stride=HEADS)].astype(bf16)
                vh[h, to, :] = (vfl[pl.ds(h, PIECE, stride=HEADS)] * seen).astype(bf16)

    def deint_range(first, last):
        @pl.loop(first, last)
        def _(j):
            deint(j)

    deint_range(0, 1)
    for u in range(4):
        reduce_cores(u)
    deint_range(1, 4)
    finish_query(0)
    finish_query(1)
    deint_range(4, 5)
    finish_query(2)
    finish_query(3)
    deint_range(5, 6)
    forward(queries, 0)
    deint_range(6, parts)
    acc[...] = jnp.zeros_like(acc)
    kself[...] = jnp.zeros_like(kself)
    vself[...] = jnp.zeros_like(vself)
    gathered(queries, 0)

    def queries_of(h):
        return qfull[h].reshape(ROWS * GROUPED, HD)

    row_request = lax.broadcasted_iota(jnp.int32, (ROWS * GROUPED, HD), 0) // (2 * UNIT)
    lane_request = lax.rem(lax.broadcasted_iota(jnp.int32, (ROWS * GROUPED, HD), 1), REQS)
    meets[...] = jnp.where((grp == 0) | (row_request == lane_request), 1.0, 0.0)

    def attend(h, j):
        mask = jnp.concatenate([meets[...]] * (CHUNK // HD), axis=1)
        for n in range(CHUNKS):
            at = pl.ds(pl.multiple_of((j * CHUNKS + n) * CHUNK, CHUNK), CHUNK)
            scores = lax.dot_general(
                queries_of(h), kh[h, at, :], (((1,), (1,)), ((), ())), preferred_element_type=f32
            )
            weights = (weights_of(scores) * mask).astype(bf16)
            values = jnp.concatenate([vh[h, at, :], ones[at, :]], axis=1)
            acc[h] += jnp.dot(weights, values, preferred_element_type=f32)

    def attend_self(h):
        scores = lax.dot_general(
            queries_of(h), kself[h], (((1,), (1,)), ((), ())), preferred_element_type=f32
        )
        index = lax.broadcasted_iota(jnp.int32, (ROWS * GROUPED, HD), 0)
        row = SHARE * (index // UNIT) + lax.rem(index, SHARE)
        key = SHARE * ctx + lax.broadcasted_iota(jnp.int32, (ROWS * GROUPED, HD), 1)
        allowed = (key <= row) & ((grp == 0) | (index // (2 * UNIT) == ctx // 2))
        weights = jnp.where(allowed, weights_of(scores), 0.0).astype(bf16)
        acc[h] += jnp.dot(weights, vself[h], preferred_element_type=f32)

    def cx3_copy(h):
        return remote(st3.at[h, other], cx3.at[h], cx3_s.at[h], cx3_r.at[h], sibling)

    def rs3_send(h, k):
        return remote(sn3.at[h, k], rs3.at[h, chip], rs3_s, rs3_r.at[h], on_chip(k))

    def rs3_all(h):
        return remote(sn3.at[h, seven], rs3.at[h, seven], rs3_s, rs3_r.at[h], sibling)

    lane8 = lax.broadcasted_iota(jnp.int32, (2 * CHIPS, 8, HD), 2) // 16

    def hand_over(h):
        num = acc[h, :, 0:HD].astype(bf16).reshape(CHIPS, 2, UNIT, HD)
        den = acc[h, :, HD:2 * HD].reshape(2 * CHIPS, 8, 8, HD)
        small = den[:, 0]
        for a in range(1, 8):
            small = jnp.where(lane8 == a, den[:, a], small)
        small = pack_den(small).reshape(CHIPS, 2, 16, HD)
        for p in range(2):
            st3[h, p, :, 0:UNIT, :] = num[:, p]
            st3[h, p, :, UNIT:MSG, :] = small[:, p]
        cx3_copy(h).start()

    def den_of(block):
        return block[:, UNIT:UNIT + 8].astype(f32) + block[:, UNIT + 8:MSG].astype(f32)

    def reduce_cores3(h):
        cx3_copy(h).wait_recv()
        mine = st3[h, core]
        got = cx3[h]
        sn3[h, :, 0:UNIT, :] = (mine[:, 0:UNIT].astype(f32) + got[:, 0:UNIT].astype(f32)).astype(bf16)
        sn3[h, :, UNIT:MSG, :] = pack_den(den_of(mine) + den_of(got))
        rs3[h, chip] = sn3[h, chip]
        for d in range(1, CHIPS):
            rs3_send(h, peer(d)).start()

    def finish_heads(h):
        rs3_all(h).wait_recv()
        got = rs3[h]
        num = jnp.sum(got[:, 0:UNIT].astype(f32), axis=0)
        den = jnp.sum(den_of(got), axis=0)
        wide = jnp.concatenate(
            [jnp.broadcast_to(den[:, 16 * a:16 * a + 1], (8, HD)) for a in range(8)], axis=0)
        hfull[h, chip, core] = (num / wide).astype(bf16)
        share_out(heads_out, h)

    def finish_kv():
        for u in range(4, 8):
            total = total1(u).astype(bf16)
            for half in range(2):
                h = 2 * (u % 2) + half
                piece = total[half * SHARE:(half + 1) * SHARE]
                if u < 6:
                    kself[h, 0:SHARE, :] = piece
                    kvfl[0, pl.ds(h, SHARE, stride=HEADS), :] = piece.astype(f32)
                else:
                    vself[h, 0:SHARE, 0:HD] = piece
                    vself[h, 0:SHARE, HD:2 * HD] = jnp.ones((SHARE, HD), bf16)
                    kvfl[1, pl.ds(h, SHARE, stride=HEADS), :] = piece.astype(f32)
        kvown[...] = kvfl[...].astype(bf16)
        remote(kvown, kvgot, gr_s, gr_r, twin).start()

    def pick_kv():
        remote(kvown, kvgot, gr_s, gr_r, twin).wait_recv()
        kvfull[0, chip, core] = jnp.where(grp == 0, kvown[...].astype(f32), kvgot[...].astype(f32)).astype(bf16)

    kv_store = pltpu.make_async_copy(kvfull.at[0], kv_out, out_sem)

    @pl.loop(0, HEADS * STEPS)
    def _(it):
        h = it // STEPS
        j = lax.rem(it, STEPS)

        @pl.when(it == 0)
        def _():
            for u in range(4, 8):
                reduce_cores(u)

        @pl.when(it == 1)
        def _():
            for u in range(1, HEADS):
                forward(queries, u)

        @pl.when((h >= 1) & (j == 0))
        def _():
            gathered(queries, h)

        @pl.when(it == 2)
        def _():
            finish_kv()
            attend_self(0)
            hand_over(0)

        @pl.when(it == 3)
        def _():
            pick_kv()
            share_out(new_rows, 0)

        @pl.when((it == 3) | (it == 4) | (it == 6))
        def _():
            reduce_cores3(it // 2 - 1)

        @pl.when(it == 5)
        def _():
            finish_heads(0)
            finish_heads(1)

        @pl.when(it == 6)
        def _():
            forward(new_rows, 0)

        @pl.when(it == 7)
        def _():
            gathered(new_rows, 0)
            kv_store.start()

        attend(h, j)

        @pl.when((h >= 1) & (j == STEPS - 1))
        def _():
            attend_self(h)
            hand_over(h)

    last = HEADS - 1
    half = ROWS // 2

    def project(h):
        heads = hfull[h, :, core]
        lhs = jnp.concatenate(
            [heads[:, 0:SHARE].reshape(half, HD), heads[:, SHARE:UNIT].reshape(half, HD)], axis=1)
        for q, w_ref in enumerate((wo_ref, wo_got)):
            term = lax.dot_general(
                lhs, w_ref[:, h * 256:(h + 1) * 256], (((1,), (1,)), ((), ())), preferred_element_type=f32)
            oacc[q] = term if h == 0 else oacc[q] + term

    reduce_cores3(last)
    finish_heads(last - 1)
    wo_copy.wait_recv()
    for h in range(last - 1):
        ag_all(heads_out, h).wait_recv()
        project(h)
    finish_heads(last)
    ag_all(heads_out, last - 1).wait_recv()
    project(last - 1)
    ag_all(heads_out, last).wait_recv()
    project(last)
    st5[...] = oacc[...].astype(bf16).reshape(2, 4, UNIT, MODEL)

    def p5_send(q, t):
        return remote(st5.at[q, t], rs5.at[4 * core + tp], p5_s, p5_r,
                      {"ctx": ctx if q == 0 else 2 * chip + other, "tp": t})

    p5_all = remote(rs5.at[seven], rs5.at[seven], p5_s, p5_r, sibling)
    for d in range(1, 4):
        to = lax.rem(tp + d, 4)
        p5_send(0, to).start()
        p5_send(1, to).start()
    p5_send(1, tp).start()
    rs5[4 * core + tp] = st5[0, tp]
    p5_all.wait_recv()
    pieces = []
    for p in range(2):
        total = rs5[4 * p].astype(f32)
        for t in range(1, 4):
            total = total + rs5[4 * p + t].astype(f32)
        pieces.append(total)
    out_ref[...] = jnp.concatenate(
        [pieces[0][0:SHARE], pieces[1][0:SHARE], pieces[0][SHARE:UNIT], pieces[1][SHARE:UNIT]], axis=0)

    @pl.loop(0, 8)
    def _(u):
        cx1_copy(u).wait_send()
        rs1_all(u).wait_send()

    @pl.loop(0, HEADS)
    def _(h):
        cx3_copy(h).wait_send()
        rs3_all(h).wait_send()
        shared_done(queries, h)
        ag_all(heads_out, h).wait_send()

    shared_done(new_rows, 0)
    remote(kvown, kvgot, gr_s, gr_r, twin).wait_send()
    wo_copy.wait_send()
    p5_all.wait_send()
    kv_store.wait()


def layer(start, lengths, tok, wq, wk, wv, wo, pool_k, pool_v):
    vmem, dma = pltpu.VMEM, pltpu.SemaphoreType.DMA
    inside = pl.BlockSpec(memory_space=pltpu.VMEM)
    outside = pl.BlockSpec(memory_space=pl.ANY)
    small = pl.BlockSpec(memory_space=pltpu.SMEM)
    share = (2 * HEADS, CHIPS, UNIT, HD)
    msg = (HEADS, CHIPS, MSG, HD)
    return pl.pallas_call(
        layer_kernel,
        name="layer",
        out_shape=(
            jax.ShapeDtypeStruct((ROWS // 4, MODEL), f32),
            jax.ShapeDtypeStruct((CHIPS, 2, 2, SHARE * HEADS, HD), bf16),
        ),
        in_specs=[small, small] + [inside] * 5 + [outside] * 2,
        out_specs=(inside, outside),
        scratch_shapes=[
            vmem((SLOTS_DEV * HEADS, HD), bf16),
            vmem((SLOTS_DEV * HEADS, HD), bf16),
            vmem((PIECE * HEADS, HD), f32),
            vmem((PIECE * HEADS, HD), f32),
            vmem((HEADS, SLOTS_DEV, HD), bf16),
            vmem((HEADS, SLOTS_DEV, HD), bf16),
            vmem((SLOTS_DEV, HD), bf16),
            vmem((HEADS, ROWS * GROUPED, 2 * HD), f32),
            vmem((ROWS * GROUPED, HD), f32),
            vmem((2 * HEADS, 2, CHIPS, UNIT, HD), bf16),
            vmem(share, bf16),
            vmem(share, bf16),
            vmem(share, bf16),
            vmem((HEADS, CHIPS, 2, UNIT, HD), bf16),
            vmem((2, SHARE * HEADS, HD), bf16),
            vmem((2, SHARE * HEADS, HD), bf16),
            vmem((1, CHIPS, 2, 2, SHARE * HEADS, HD), bf16),
            vmem((HEADS, HD, HD), bf16),
            vmem((HEADS, HD, 2 * HD), bf16),
            vmem((2, SHARE * HEADS, HD), f32),
            vmem((HEADS, 2, CHIPS, MSG, HD), bf16),
            vmem(msg, bf16),
            vmem(msg, bf16),
            vmem(msg, bf16),
            vmem((HEADS, CHIPS, 2, UNIT, HD), bf16),
            vmem((MODEL, HEADS * GROUPED * HD), bf16),
            vmem((2, ROWS // 2, MODEL), f32),
            vmem((2, 4, UNIT, MODEL), bf16),
            vmem((8, UNIT, MODEL), bf16),
            dma((2, SLOTS_DEV // DEINT)),
            dma(()),
            dma((8,)), dma((8,)),
            dma(()), dma((8,)),
            dma(()), dma((HEADS,)), dma((HEADS,)), dma((HEADS,)),
            dma(()), dma((1,)), dma((1,)), dma((1,)),
            dma(()), dma((HEADS,)),
            dma(()), dma(()),
            dma(()), dma(()),
            dma((HEADS,)), dma((HEADS,)),
            dma(()), dma((HEADS,)),
            dma(()), dma(()),
        ],
        compiler_params=pltpu.CompilerParams(
            collective_id=0, has_side_effects=True, vmem_limit_bytes=60 * 2**20),
        cost_estimate=pl.CostEstimate(
            flops=22 * 10**9, bytes_accessed=14 * 2**20, transcendentals=42 * 10**6),
    )(start, lengths, tok, wq, wk, wv, wo, pool_k, pool_v)


COPIES = 8


def store_kernel(
    start_ref, dest_ref, attn, kv, pool_k, pool_v, attn_out, keys_out, values_out, held, in_sem, copy_sem, row_sem
):
    grp = lax.axis_index("grp")
    first = lax.axis_index("ctx") * SLOTS_DEV
    span = SLOTS_DEV // COPIES

    def fetch(which, i):
        at = pl.ds(i * span, span)
        return pltpu.make_async_copy((pool_k, pool_v)[which].at[at], held.at[which, at], in_sem.at[which, i])

    def put(which, i):
        at = pl.ds(i * span, span)
        return pltpu.make_async_copy(held.at[which, at], (keys_out, values_out)[which].at[at], copy_sem.at[which, i])

    for i in range(COPIES):
        for which in range(2):
            fetch(which, i).start()
    attn_out[...] = attn[...].T.astype(bf16)
    for i in range(COPIES):
        for which in range(2):
            fetch(which, i).wait()
            put(which, i).start()
    for i in range(COPIES):
        for which in range(2):
            put(which, i).wait()

    def slot(b):
        return jnp.where(grp == 0, start_ref[0] + b * BLK, dest_ref[b] * BLK) - first

    def block(b, which):
        dst = (keys_out, values_out)[which]
        return pltpu.make_async_copy(
            kv.at[b // 4, lax.rem(b // 2, 2), which, pl.ds(lax.rem(b, 2) * BLK, BLK)],
            dst.at[pl.ds(slot(b), BLK)], row_sem.at[which, b])

    def inside(b):
        at = slot(b)
        return (at >= 0) & (at <= SLOTS_DEV - BLK)

    def across(b):
        at = slot(b)
        return ((at > -BLK) & (at < 0)) | ((at > SLOTS_DEV - BLK) & (at < SLOTS_DEV))

    blocks = ROWS // BLK

    @pl.loop(0, blocks)
    def _(b):
        @pl.when(inside(b))
        def _():
            block(b, 0).start()
            block(b, 1).start()

        @pl.when(across(b))
        def _():
            @pl.loop(0, BLK)
            def _(i):
                at = slot(b) + i

                @pl.when((at >= 0) & (at < SLOTS_DEV))
                def _():
                    for which in range(2):
                        row = pltpu.make_async_copy(
                            kv.at[b // 4, lax.rem(b // 2, 2), which,
                                  pl.ds(lax.rem(b, 2) * BLK + i, 1)],
                            (keys_out, values_out)[which].at[pl.ds(at, 1)],
                            row_sem.at[which, b])
                        row.start()
                        row.wait()

    @pl.loop(0, blocks)
    def _(b):
        @pl.when(inside(b))
        def _():
            block(b, 0).wait()
            block(b, 1).wait()


def store(start, dest_blocks, attn, kv, pool_k, pool_v):
    dma = pltpu.SemaphoreType.DMA
    inside = pl.BlockSpec(memory_space=pltpu.VMEM)
    outside = pl.BlockSpec(memory_space=pl.ANY)
    small = pl.BlockSpec(memory_space=pltpu.SMEM)
    shape = jax.ShapeDtypeStruct((SLOTS_DEV, HEADS, HD), bf16)
    return pl.pallas_call(
        store_kernel,
        name="store",
        out_shape=(jax.ShapeDtypeStruct((MODEL, ROWS // 4), bf16), shape, shape),
        in_specs=[small, small, inside] + [outside] * 3,
        out_specs=(inside, outside, outside),
        scratch_shapes=[
            pltpu.VMEM((2, SLOTS_DEV, HEADS, HD), bf16),
            dma((2, COPIES)), dma((2, COPIES)), dma((2, ROWS // BLK))],
        compiler_params=pltpu.CompilerParams(vmem_limit_bytes=60 * 2**20),
        cost_estimate=pl.CostEstimate(flops=0, bytes_accessed=21 * 2**20, transcendentals=0),
    )(start, dest_blocks, attn, kv, pool_k, pool_v)


def body(
    new_tokens, w_query, w_key, w_value, w_out, pool_keys, pool_values, stretch_start, lengths, dest_blocks
):
    flat = (SLOTS_DEV * HEADS, HD)
    pool_k = pool_keys.reshape(flat)
    pool_v = pool_values.reshape(flat)
    out, kv = layer(
        stretch_start, lengths, new_tokens[0].T, w_query, w_key, w_value, w_out.T, pool_k, pool_v)
    kv = kv.reshape(CHIPS, 2, 2, SHARE, HEADS, HD)
    attn_out, keys_out, values_out = store(
        stretch_start, dest_blocks, out, kv, pool_keys[0], pool_values[0])
    return attn_out.T[None], keys_out[None], values_out[None]


def solution(mesh):
    return jax.shard_map(
        body,
        mesh=mesh,
        in_specs=(
            P("grp", None, "ctx"),
            P("ctx", "tp"),
            P("ctx", "tp"),
            P("ctx", "tp"),
            P("tp", "ctx"),
            P("grp", "ctx", "tp", None),
            P("grp", "ctx", "tp", None),
            P(),
            P(),
            P(),
        ),
        out_specs=(P("grp", "tp", "ctx"), P("grp", "ctx", "tp", None), P("grp", "ctx", "tp", None)),
        check_vma=False,
    )
```

time: 456 us -> 116 us (0.25)
  the two profiles are of different devices: /device:TPU:56 before, /device:TPU:57 now
where the time goes in v2:
time: 116 us
  Pallas kernels  115 us (99%)
  between operations  1.29 us (1%)
    pallas_call x1, Pallas kernels, layer(): pl.pallas_call(layer_kernel, name='layer', out_shape=(jax.ShapeDtypeStruc...  71.8 us
    pallas_call x1, Pallas kernels, store(): pl.pallas_call(store_kernel, name='store', out_shape=(jax.ShapeDtypeStruc...  43.1 us

profile of v2, /device:TPU:57, one launch (start us, length us, event | category | flops | bytes accessed | tf_op | source)
XLA Modules:
  0.0 116.2 jit_solution(18087089465552096834)
XLA Ops:
  1.3 71.8 %layer.1 = (f32[128,288]{1,0:T(8,128)}, bf16[8,2,2,128,128]{4,3,2,1,0:T(8,128)(2,1)}) custom-call(s32[1]{0:T(128)S(6)} %copy.13.start_ref, s32[8]{0:T(128)} %len_ref.1, bf16[288,512]{1,0:T(8,128)(2,1)} %bitcast.22, bf16[288,1024]{1,0:T(8,128)(2,1)} %wq_ref.1, bf16[288,512]{1,0:T(8,128)(2,1)} %wk_ref.1, bf16[288,512]{1,0:T(8,128)(2,1)} %wv_ref.1, ...), custom_call_target="tpu_custom_call" | custom-call | flops 22000001024 | bytes 14680064 | tf_op jit(solution)/shard_map/layer/pallas_call | solution.py:457
  73.1 43.1 %store.1 = (bf16[288,128]{1,0:T(8,128)(2,1)}, bf16[5120,4,128]{2,1,0:T(4,128)(2,1)}, bf16[5120,4,128]{2,1,0:T(4,128)(2,1)}) custom-call(s32[1]{0:T(128)S(6)} %copy.13.start_ref, s32[32]{0:T(128)} %dest_ref.1, f32[128,288]{1,0:T(8,128)} %get-tuple-element.8.attn, bf16[8,2,2,32,4,128]{5,4,3,2,1,0:T(4,128)(2,1)} %bitcast.18, bf16[5120,4,128]{2,1,0:T(4,128)(2,1)} %bitcast.15, ...), custom_call_target="tpu_custom_call" | custom-call | bytes 22020096 | tf_op jit(solution)/shard_map/store/pallas_call | solution.py:603

commit v3 on v2

--- a/solution.py
+++ b/solution.py
@@ -223,6 +223,8 @@
     finish_query(2)
     finish_query(3)
     deint_range(5, 6)
+    for u in range(4, 8):
+        reduce_cores(u)
     forward(queries, 0)
     deint_range(6, parts)
     acc[...] = jnp.zeros_like(acc)
@@ -332,11 +334,6 @@
         h = it // STEPS
         j = lax.rem(it, STEPS)
 
-        @pl.when(it == 0)
-        def _():
-            for u in range(4, 8):
-                reduce_cores(u)
-
         @pl.when(it == 1)
         def _():
             for u in range(1, HEADS):
@@ -346,34 +343,30 @@
         def _():
             gathered(queries, h)
 
-        @pl.when(it == 2)
+        @pl.when(it == 3)
         def _():
             finish_kv()
             attend_self(0)
             hand_over(0)
 
-        @pl.when(it == 3)
+        @pl.when(it == 4)
+        def _():
+            reduce_cores3(0)
+            reduce_cores3(1)
+
+        @pl.when(it == 6)
+        def _():
+            reduce_cores3(2)
+
+        @pl.when(it == 5)
         def _():
             pick_kv()
             share_out(new_rows, 0)
 
-        @pl.when((it == 3) | (it == 4) | (it == 6))
-        def _():
-            reduce_cores3(it // 2 - 1)
-
-        @pl.when(it == 5)
-        def _():
-            finish_heads(0)
-            finish_heads(1)
-
-        @pl.when(it == 6)
-        def _():
-            forward(new_rows, 0)
-
-        @pl.when(it == 7)
-        def _():
-            gathered(new_rows, 0)
-            kv_store.start()
+        @pl.when((it == 6) | (it == 7))
+        def _():
+            finish_heads(it - 6)
+
 
         attend(h, j)
 
@@ -396,6 +389,7 @@
 
     reduce_cores3(last)
     finish_heads(last - 1)
+    forward(new_rows, 0)
     wo_copy.wait_recv()
     for h in range(last - 1):
         ag_all(heads_out, h).wait_recv()
@@ -418,6 +412,8 @@
         p5_send(1, to).start()
     p5_send(1, tp).start()
     rs5[4 * core + tp] = st5[0, tp]
+    gathered(new_rows, 0)
+    kv_store.start()
     p5_all.wait_recv()
     pieces = []
     for p in range(2):
@@ -517,7 +513,7 @@
 
 
 def store_kernel(
-    start_ref, dest_ref, attn, kv, pool_k, pool_v, attn_out, keys_out, values_out, held, in_sem, copy_sem, row_sem
+    start_ref, dest_ref, attn, kv, pool_k, pool_v, attn_out, keys_out, values_out, held, rows, kv_sem, in_sem, copy_sem, row_sem
 ):
     grp = lax.axis_index("grp")
     first = lax.axis_index("ctx") * SLOTS_DEV
@@ -534,6 +530,8 @@
     for i in range(COPIES):
         for which in range(2):
             fetch(which, i).start()
+    take = pltpu.make_async_copy(kv, rows, kv_sem)
+    take.start()
     attn_out[...] = attn[...].T.astype(bf16)
     for i in range(COPIES):
         for which in range(2):
@@ -542,6 +540,7 @@
     for i in range(COPIES):
         for which in range(2):
             put(which, i).wait()
+    take.wait()
 
     def slot(b):
         return jnp.where(grp == 0, start_ref[0] + b * BLK, dest_ref[b] * BLK) - first
@@ -549,7 +548,7 @@
     def block(b, which):
         dst = (keys_out, values_out)[which]
         return pltpu.make_async_copy(
-            kv.at[b // 4, lax.rem(b // 2, 2), which, pl.ds(lax.rem(b, 2) * BLK, BLK)],
+            rows.at[b // 4, lax.rem(b // 2, 2), which, pl.ds(lax.rem(b, 2) * BLK, BLK)],
             dst.at[pl.ds(slot(b), BLK)], row_sem.at[which, b])
 
     def inside(b):
@@ -579,7 +578,7 @@
                 def _():
                     for which in range(2):
                         row = pltpu.make_async_copy(
-                            kv.at[b // 4, lax.rem(b // 2, 2), which,
+                            rows.at[b // 4, lax.rem(b // 2, 2), which,
                                   pl.ds(lax.rem(b, 2) * BLK + i, 1)],
                             (keys_out, values_out)[which].at[pl.ds(at, 1)],
                             row_sem.at[which, b])
@@ -608,6 +607,7 @@
         out_specs=(inside, outside, outside),
         scratch_shapes=[
             pltpu.VMEM((2, SLOTS_DEV, HEADS, HD), bf16),
+            pltpu.VMEM(kv.shape, bf16), dma(()),
             dma((2, COPIES)), dma((2, COPIES)), dma((2, ROWS // BLK))],
         compiler_params=pltpu.CompilerParams(vmem_limit_bytes=60 * 2**20),
         cost_estimate=pl.CostEstimate(flops=0, bytes_accessed=21 * 2**20, transcendentals=0),

time: 116 us -> 94.6 us (0.82)
  the two profiles are of different devices: /device:TPU:57 before, /device:TPU:56 now
where the time goes in v3:
time: 94.6 us; the launch traced here: 94.5 us
  Pallas kernels  93.2 us (99%)
  between operations  1.29 us (1%)
    pallas_call x1, Pallas kernels, layer(): pl.pallas_call(layer_kernel, name='layer', out_shape=(jax.ShapeDtypeStruc...  66.8 us
    pallas_call x1, Pallas kernels, store(): pl.pallas_call(store_kernel, name='store', out_shape=(jax.ShapeDtypeStruc...  26.3 us

profile of v3, /device:TPU:56, one launch (start us, length us, event | category | flops | bytes accessed | tf_op | source)
XLA Modules:
  0.0 94.5 jit_solution(2627747987218207076)
XLA Ops:
  1.3 66.8 %layer.1 = (f32[128,288]{1,0:T(8,128)}, bf16[8,2,2,128,128]{4,3,2,1,0:T(8,128)(2,1)}) custom-call(s32[1]{0:T(128)S(6)} %copy.13.start_ref, s32[8]{0:T(128)} %len_ref.1, bf16[288,512]{1,0:T(8,128)(2,1)} %bitcast.22, bf16[288,1024]{1,0:T(8,128)(2,1)} %wq_ref.1, bf16[288,512]{1,0:T(8,128)(2,1)} %wk_ref.1, bf16[288,512]{1,0:T(8,128)(2,1)} %wv_ref.1, ...), custom_call_target="tpu_custom_call" | custom-call | flops 22000001024 | bytes 14680064 | tf_op jit(solution)/shard_map/layer/pallas_call | solution.py:453
  68.1 26.3 %store.1 = (bf16[288,128]{1,0:T(8,128)(2,1)}, bf16[5120,4,128]{2,1,0:T(4,128)(2,1)}, bf16[5120,4,128]{2,1,0:T(4,128)(2,1)}) custom-call(s32[1]{0:T(128)S(6)} %copy.13.start_ref, s32[32]{0:T(128)} %dest_ref.1, f32[128,288]{1,0:T(8,128)} %get-tuple-element.8.attn, bf16[8,2,2,32,4,128]{5,4,3,2,1,0:T(4,128)(2,1)} %bitcast.18, bf16[5120,4,128]{2,1,0:T(4,128)(2,1)} %bitcast.15, ...), custom_call_target="tpu_custom_call" | custom-call | bytes 22020096 | tf_op jit(solution)/shard_map/store/pallas_call | solution.py:602

commit v4 on v3

--- a/solution.py
+++ b/solution.py
@@ -18,8 +18,8 @@
 MSG = UNIT + 16
 DEINT = 512
 PIECE = 128
-CHUNK = 1280
-CHUNKS = 2
+CHUNK = 512
+CHUNKS = 5
 STEPS = SLOTS_DEV // (CHUNK * CHUNKS)
 MODEL = 288
 LOG2E = 1.4426950408889634
@@ -509,7 +509,7 @@
     )(start, lengths, tok, wq, wk, wv, wo, pool_k, pool_v)
 
 
-COPIES = 8
+COPIES = 4
 
 
 def store_kernel(
@@ -549,7 +549,7 @@
         dst = (keys_out, values_out)[which]
         return pltpu.make_async_copy(
             rows.at[b // 4, lax.rem(b // 2, 2), which, pl.ds(lax.rem(b, 2) * BLK, BLK)],
-            dst.at[pl.ds(slot(b), BLK)], row_sem.at[which, b])
+            dst.at[pl.ds(slot(b), BLK)], row_sem.at[which])
 
     def inside(b):
         at = slot(b)
@@ -581,7 +581,7 @@
                             rows.at[b // 4, lax.rem(b // 2, 2), which,
                                   pl.ds(lax.rem(b, 2) * BLK + i, 1)],
                             (keys_out, values_out)[which].at[pl.ds(at, 1)],
-                            row_sem.at[which, b])
+                            row_sem.at[which])
                         row.start()
                         row.wait()
 
@@ -608,7 +608,7 @@
         scratch_shapes=[
             pltpu.VMEM((2, SLOTS_DEV, HEADS, HD), bf16),
             pltpu.VMEM(kv.shape, bf16), dma(()),
-            dma((2, COPIES)), dma((2, COPIES)), dma((2, ROWS // BLK))],
+            dma((2, COPIES)), dma((2, COPIES)), dma((2,))],
         compiler_params=pltpu.CompilerParams(vmem_limit_bytes=60 * 2**20),
         cost_estimate=pl.CostEstimate(flops=0, bytes_accessed=21 * 2**20, transcendentals=0),
     )(start, dest_blocks, attn, kv, pool_k, pool_v)

time: 94.6 us -> 82.5 us (0.87)
  the two profiles are of different devices: /device:TPU:56 before, /device:TPU:1 now
where the time goes in v4:
time: 82.5 us; the launch traced here: 82.4 us
  Pallas kernels  81.1 us (98%)
  between operations  1.29 us (2%)
    pallas_call x1, Pallas kernels, layer(): pl.pallas_call(layer_kernel, name='layer', out_shape=(jax.ShapeDtypeStruc...  70.8 us
    pallas_call x1, Pallas kernels, store(): pl.pallas_call(store_kernel, name='store', out_shape=(jax.ShapeDtypeStruc...  10.3 us

profile of v4, /device:TPU:1, one launch (start us, length us, event | category | flops | bytes accessed | tf_op | source)
XLA Modules:
  0.0 82.4 jit_solution(7591160211772206297)
XLA Ops:
  1.3 70.8 %layer.1 = (f32[128,288]{1,0:T(8,128)}, bf16[8,2,2,128,128]{4,3,2,1,0:T(8,128)(2,1)}) custom-call(s32[1]{0:T(128)S(6)} %copy.13.start_ref, s32[8]{0:T(128)} %len_ref.1, bf16[288,512]{1,0:T(8,128)(2,1)} %bitcast.22, bf16[288,1024]{1,0:T(8,128)(2,1)} %wq_ref.1, bf16[288,512]{1,0:T(8,128)(2,1)} %wk_ref.1, bf16[288,512]{1,0:T(8,128)(2,1)} %wv_ref.1, ...), custom_call_target="tpu_custom_call" | custom-call | flops 22000001024 | bytes 14680064 | tf_op jit(solution)/shard_map/layer/pallas_call | solution.py:453
  72.1 10.3 %store.1 = (bf16[288,128]{1,0:T(8,128)(2,1)}, bf16[5120,4,128]{2,1,0:T(4,128)(2,1)}, bf16[5120,4,128]{2,1,0:T(4,128)(2,1)}) custom-call(s32[1]{0:T(128)S(6)} %copy.13.start_ref, s32[32]{0:T(128)} %dest_ref.1, f32[128,288]{1,0:T(8,128)} %get-tuple-element.8.attn, bf16[8,2,2,32,4,128]{5,4,3,2,1,0:T(4,128)(2,1)} %bitcast.18, bf16[5120,4,128]{2,1,0:T(4,128)(2,1)} %bitcast.15, ...), custom_call_target="tpu_custom_call" | custom-call | bytes 22020096 | tf_op jit(solution)/shard_map/store/pallas_call | solution.py:602
